TPU v7x, 32 devices: a whole 2x2x4 slice. The times are simulated.
32 devices in a mesh: pb: 16 (over z, y, x), ga: 2 (over core).
Axes of the slice: x: 2, y: 2, z: 4, core: 2. Of those that a mesh axis runs over, the one named last changes fastest.
Arguments:
- q_of_pair: int32 [4096, 1], P('pb'), may hold values from 0 to 31; in each aligned block of 256 rows (0 to 255, 256 to 511, ...) at most 12 rows name the same one
- q_slot: int32 [32], replicated, may hold values from 0 to 31, each once
- valence: bfloat16 [4096, 16, 1024], P('pb', None, 'ga'), may hold values from -6 to 6
- conduction: bfloat16 [4096, 16, 1024], P('pb', None, 'ga'), may hold values from -0.1875 to 0.1875
- screened: bfloat16 [32, 1024, 1024], P('pb', 'ga'), may hold values from -0.1875 to 0.1875
Outputs:
- kernel_blocks: float32 [4096, 256], P('pb', 'ga')
Inputs may be any that keep to these rules, and one draw needn't show every extreme that they name: `q_of_pair`: among the k-pairs of one index of pb (aligned blocks of 256 rows) no q appears more than 12 times, and some q appears exactly 12 times. `q_slot`: each slot is taken by exactly one q.
All inputs are finite; a program needn't handle non-finite values.
Results may differ from a plain program's by a relative error of at most 0.0029.
Values may be sent and summed in bfloat16 or wider, within the bound.
A program may use at most 128 MiB of HBM per device.

v0:
```python
import jax
import jax.numpy as jnp
from jax import lax
from jax.sharding import PartitionSpec as P


def body(q_of_pair, q_slot, valence, conduction, screened):
    peer_count = lax.axis_size("pb")
    pair_count = q_of_pair.shape[0]
    local_count = screened.shape[0]
    q_total = q_slot.shape[0]
    capacity = max(2, (3 * pair_count + 2 * q_total - 1) // (2 * q_total))
    slot_span = local_count * capacity
    band_pairs = valence.shape[1]
    q_ids = q_of_pair[:, 0]
    q_match = (q_ids[:, None] == jnp.arange(q_total, dtype=jnp.int32)[None, :]).astype(jnp.int32)
    slot_index = jnp.sum(q_match * q_slot[None, :], axis=1)
    order_row = jnp.arange(pair_count, dtype=jnp.int32)
    same_q = (q_ids[:, None] == q_ids[None, :]) & (order_row[None, :] < order_row[:, None])
    rank_in_q = jnp.sum(same_q.astype(jnp.int32), axis=1)
    target = slot_index // local_count * slot_span + slot_index % local_count * capacity + rank_in_q
    hit_table = (
        target[None, :] == jnp.arange(peer_count * slot_span, dtype=jnp.int32)[:, None]
    ).astype(jnp.int32)
    source_row = jnp.sum(hit_table * order_row[None, :], axis=1)
    filled = jnp.sum(hit_table, axis=1) > 0

    def pack_rows(values):
        rows = jnp.take(values, source_row, axis=0)
        rows = jnp.where(filled[:, None, None], rows, jnp.zeros_like(rows))
        return rows.reshape((peer_count, slot_span) + values.shape[1:])

    cond_recv, val_recv = (
        lax.all_to_all(pack_rows(conduction), "pb", split_axis=0, concat_axis=0, tiled=True),
        lax.all_to_all(pack_rows(valence), "pb", split_axis=0, concat_axis=0, tiled=True),
    )
    val_recv = lax.all_gather(val_recv, "ga", axis=3, tiled=True)
    val_recv = val_recv.reshape(peer_count, local_count, capacity, band_pairs, val_recv.shape[-1])
    cond_recv = cond_recv.reshape(
        peer_count, local_count, capacity, band_pairs, cond_recv.shape[-1]
    )
    applied = jnp.einsum(
        "lgh,plabh->plabg", screened, val_recv, preferred_element_type=jnp.float32
    ).astype(jnp.bfloat16)
    partial_value = jnp.einsum(
        "placg,plabg->placb", cond_recv, applied, preferred_element_type=jnp.float32
    )
    partial_value = partial_value.reshape(peer_count, slot_span, band_pairs * band_pairs)
    summed = lax.psum(partial_value, "ga")
    half_width = summed.shape[2] // lax.axis_size("ga")
    my_share = lax.dynamic_slice_in_dim(summed, lax.axis_index("ga") * half_width, half_width, 2)
    returned = lax.all_to_all(my_share, "pb", split_axis=0, concat_axis=0, tiled=True)
    return jnp.take(returned.reshape(peer_count * slot_span, returned.shape[-1]), target, axis=0)


def solution(mesh):
    in_specs = (P("pb", None), P(), P("pb", None, "ga"), P("pb", None, "ga"), P("pb", "ga", None))
    out_specs = P("pb", "ga")
    return jax.shard_map(body, mesh=mesh, in_specs=in_specs, out_specs=out_specs, check_vma=False)
```

profile of v0, /device:TPU:0, one launch (start us, length us, event | category | flops | bytes accessed | tf_op | source)
XLA Modules:
  0.0 379.1 jit_solution(3839703365392103992)
XLA Ops:
  6.5 0.0 copy-start
  6.5 0.0 all-gather.2.cloned.1.call-start
  6.5 1.0 convert_reduce_fusion.1
  7.6 0.8 select_reduce_fusion.1
  8.4 0.2 convert_reduce_fusion
  8.6 5.9 %gather_fusion.2 = bf16[384,16,512]{2,1,0:T(8,128)(2,1)} fusion(bf16[256,16,512]{2,1,0:T(8,128)(2,1)} %param.9, s32[1024]{0:T(1024)S(1)} %pad_clamp_fusion.1), kind=kCustom, calls=%fused_computation.1.clone | custom fusion | bytes 12584448 | tf_op jit(solution)/shard_map/jit(_take)/gather | solution.py:29
  14.5 5.8 %gather_fusion.1 = bf16[384,16,512]{2,1,0:T(8,128)(2,1)} fusion(bf16[256,16,512]{2,1,0:T(8,128)(2,1)} %param.10, s32[1024]{0:T(1024)S(1)} %pad_clamp_fusion.1), kind=kCustom, calls=%fused_computation.clone | custom fusion | bytes 12584448 | tf_op jit(solution)/shard_map/jit(_take)/gather | solution.py:29
  20.3 9.3 %select_select_fusion = (bf16[384,16,512]{2,1,0:T(8,128)(2,1)S(1)}, bf16[384,16,512]{2,1,0:T(8,128)(2,1)}) fusion(bf16[384,16,512]{2,1,0:T(8,128)(2,1)} %gather_fusion.2, pred[384]{0:T(512)(128)(4,1)S(1)} %get-tuple-element.12, pred[384]{0:T(512)(128)(4,1)S(1)} %get-tuple-element.13, bf16[384,16,512]{2,1,0:T(8,128)(2,1)} %gather_fusion.1), kind=kLoop, calls=%fused_computation.5 | loop fusion | flops 12582912 | bytes 25166592 | tf_op jit(solution)/shard_map/jit(_where)/select_n | solution.py:30
  29.6 146.9 %all_to_all.15 = bf16[16,24,16,512]{3,2,1,0:T(8,128)(2,1)} all-to-all(bf16[16,24,16,512]{3,2,1,0:T(8,128)(2,1)S(1)} %bitcast.23), channel_id=1, replica_groups=mesh['pb'=16,'ga'=2] {'pb'}, dimensions={0} | all-to-all | bytes 12582912 | tf_op jit(solution)/shard_map/all_to_all | solution.py:35
  176.5 0.0 all-gather.2.cloned.1.call-update
  176.6 0.0 all-reduce.2.cloned.1.call-start
  176.6 142.0 %all_to_all.16 = bf16[16,24,16,512]{3,2,1,0:T(8,128)(2,1)} all-to-all(bf16[16,24,16,512]{3,2,1,0:T(8,128)(2,1)} %bitcast.22), channel_id=1, replica_groups=mesh['pb'=16,'ga'=2] {'pb'}, dimensions={0} | all-to-all | bytes 12582912 | tf_op jit(solution)/shard_map/all_to_all | solution.py:34
  318.6 0.0 all-gather.2.cloned.1.call-done
  318.6 0.0 copy-done
  318.6 14.2 %fusion = f32[16,2,12,16,16]{4,3,2,1,0:T(8,128)} fusion(bf16[16,2,12,16,512]{4,3,2,1,0:T(8,128)(2,1)} %bitcast.25, bf16[16,2,12,16,1024]{4,3,2,1,0:T(8,128)(2,1)} %bitcast.31, bf16[2,512,1024]{2,1,0:T(8,128)(2,1)S(1)} %copy-done), kind=kOutput, calls=%fused_computation.3 | convolution fusion | flops 6546259968 | bytes 21364736 | tf_op jit(solution)/shard_map/placg,plabg->placb/dot_general | solution.py:45
  332.9 3.5 reshape.165
  336.3 0.0 all-reduce.2.cloned.1.call-update
  336.4 16.9 %all-reduce.2.cloned.1.call-done = f32[16,24,256]{2,1,0:T(8,128)} async-done(((f32[16,24,256]{2,1,0:T(8,128)}), f32[16,24,256]{2,1,0:T(8,128)}) %all-reduce.2.cloned.1.call-update) | async-done | bytes 393232 | tf_op jit(solution)/shard_map/psum | solution.py:49
  353.3 1.6 constant_dynamic-slice_fusion
  354.9 6.8 %all-to-all-start.2 = ((f32[16,24,128]{2,1,0:T(8,128)}), f32[16,24,128]{2,1,0:T(8,128)S(1)}, u32[]{:S(2)}, u32[]{:S(2)}) async-start(f32[16,24,128]{2,1,0:T(8,128)} %constant_dynamic-slice_fusion), calls=%async_computation.2 | async-start | bytes 393216 | tf_op jit(solution)/shard_map/all_to_all | solution.py:52
  361.7 9.1 %all-to-all-done.2 = f32[16,24,128]{2,1,0:T(8,128)S(1)} async-done(((f32[16,24,128]{2,1,0:T(8,128)}), f32[16,24,128]{2,1,0:T(8,128)S(1)}, u32[]{:S(2)}, u32[]{:S(2)}) %all-to-all-start.2) | async-done | bytes 196640 | tf_op jit(solution)/shard_map/all_to_all | solution.py:52
  370.8 0.7 gather_fusion
  371.5 0.8 broadcast_select_fusion
  (6 shorter events, 0.1 us)
Async XLA Ops:
  6.5 312.1 %copy-start = (bf16[2,512,1024]{2,1,0:T(8,128)(2,1)S(1)}, bf16[2,512,1024]{2,1,0:T(8,128)(2,1)}, u32[]{:S(2)}) copy-start(bf16[2,512,1024]{2,1,0:T(8,128)(2,1)} %param.11) | copy-start | bytes 6291460
  6.5 312.1 %all-gather.2.cloned.1.call-start = ((), (), s32[]{:S(2)}) async-start(), calls=%async_computation.3 | async-start | bytes 18874368 | tf_op jit(solution)/shard_map/all_gather | solution.py:37
  176.6 176.7 %all-reduce.2.cloned.1.call-start = ((), (), s32[]{:S(2)}) async-start(), calls=%async_computation.4 | async-start | bytes 786432 | tf_op jit(solution)/shard_map/psum | solution.py:49
  354.9 15.9 %all-to-all-start.2 = ((f32[16,24,128]{2,1,0:T(8,128)}), f32[16,24,128]{2,1,0:T(8,128)S(1)}, u32[]{:S(2)}, u32[]{:S(2)}) async-start(f32[16,24,128]{2,1,0:T(8,128)} %constant_dynamic-slice_fusion), calls=%async_computation.2 | async-start | bytes 393216 | tf_op jit(solution)/shard_map/all_to_all | solution.py:52
Sparse Core Ops, SparseCore 0:
  176.7 23.1 all-gather.1
  336.5 16.7 all-reduce.1
where the time goes:
time: 380 us; the launch traced here: 379 us
  blocking collectives  289 us (76%)
  waiting for transfers between devices  26 us (7%)
  local copies, waits for them, and re-layouts  17.5 us (5%)
  matrix products  14.2 us (4%)
  between operations  13.5 us (4%)
  other arithmetic  12.2 us (3%)
  starting transfers between devices  6.83 us (2%)
    all_to_all x1, blocking collectives, body(): lax.all_to_all(pack_rows(valence), 'pb', split_axis=0, concat_axis=0, til...  147 us
    all_to_all x1, blocking collectives, body(): lax.all_to_all(pack_rows(conduction), 'pb', split_axis=0, concat_axis=0,...  142 us
    psum x1, waiting for transfers between devices, body(): summed = lax.psum(partial_value, 'ga')  16.9 us
    dot_general x1, matrix products, body(): jnp.einsum('placg,plabg->placb', cond_recv, applied, preferred_element_ty...  14.2 us
    gather x2, local copies, waits for them, and re-layouts, pack_rows(): rows = jnp.take(values, source_row, axis=0)  11.7 us
    select_n x1, other arithmetic, pack_rows(): rows = jnp.where(filled[:, None, None], rows, jnp.zeros_like(rows))  9.32 us
    all_to_all x1, waiting for transfers between devices, body(): lax.all_to_all(my_share, 'pb', split_axis=0, concat_axis=0, tiled=True)  9.06 us
  transfers between devices with their start and end apart: 3, of which 2 were waited for; matrix products, arithmetic and copies ran while one was open for 0% of the time, Pallas kernels for 0%

commit v1 on v0

v1 whole, which is shorter than its diff:
```python
import functools

import jax
import jax.numpy as jnp
from jax import lax
from jax.experimental import pallas as pl
from jax.experimental.pallas import tpu as pltpu
from jax.sharding import PartitionSpec as P

MESH = pl.DeviceIdType.MESH


def kernel(outer, inner, local, cap, cap_pad, steps,
           source_row, target, val_hbm, cond_hbm, w_hbm, out_ref,
           val_in, cond_in, pack_v, pack_c, vbuf, cbuf, wbuf, app, part, sib, back, ret,
           in_sem, w_up, w_down, w_recv, v_send, c_send, v_recv, c_recv,
           s_send, s_recv, p_sem, r_send, r_recv):
    me = lax.axis_index("pb")
    core = lax.axis_index("ga")
    line, place = me // inner, lax.rem(me, inner)
    bands = val_in.shape[1]
    rows = cap * bands
    slots = outer * local
    half = val_in.shape[2]

    def peer(to_line, to_place):
        return (to_line * inner + to_place, core)

    sibling = (me, 1 - core)

    def slot_at(step):
        found = jnp.int32(0)
        for z in range(outer):
            for k, j in enumerate(steps[z]):
                found = jnp.where((line == z) & (step == k), jnp.int32(j), found)
        return found

    barrier = pltpu.get_barrier_semaphore()
    pl.semaphore_signal(barrier, inc=1, device_id=sibling, device_id_type=MESH)
    for d in range(1, inner):
        pl.semaphore_signal(barrier, inc=1, device_id=peer(line, lax.rem(place + d, inner)),
                            device_id_type=MESH)

    @pl.when(line > 0)
    def _():
        pl.semaphore_signal(barrier, inc=1, device_id=peer(line - 1, place), device_id_type=MESH)

    @pl.when(line < outer - 1)
    def _():
        pl.semaphore_signal(barrier, inc=1, device_id=peer(line + 1, place), device_id_type=MESH)

    copy_val = pltpu.make_async_copy(val_hbm, val_in, in_sem.at[0])
    copy_cond = pltpu.make_async_copy(cond_hbm, cond_in, in_sem.at[1])
    copy_w = pltpu.make_async_copy(w_hbm, wbuf.at[pl.ds(line * local, local)], in_sem.at[2])
    copy_w.start()
    copy_val.start()
    copy_cond.start()
    app[...] = jnp.zeros_like(app)
    copy_w.wait()
    pl.semaphore_wait(barrier, inner + (line > 0).astype(jnp.int32)
                      + (line < outer - 1).astype(jnp.int32))

    def w_copy(j, to_line, send):
        return pltpu.make_async_remote_copy(
            src_ref=wbuf.at[j], dst_ref=wbuf.at[j], send_sem=send.at[j],
            recv_sem=w_recv.at[j], device_id=peer(to_line, place), device_id_type=MESH)

    for l in range(local):
        @pl.when(line < outer - 1)
        def _():
            w_copy(line * local + l, line + 1, w_up).start()

        @pl.when(line > 0)
        def _():
            w_copy(line * local + l, line - 1, w_down).start()

    def v_copy(j, to, frm):
        return pltpu.make_async_remote_copy(
            src_ref=pack_v.at[to, j], dst_ref=vbuf.at[core, j, frm],
            send_sem=v_send.at[to * slots + j], recv_sem=v_recv.at[frm * slots + j],
            device_id=peer(line, to), device_id_type=MESH)

    def c_copy(j, to, frm):
        return pltpu.make_async_remote_copy(
            src_ref=pack_c.at[to, j], dst_ref=cbuf.at[j, frm],
            send_sem=c_send.at[to * slots + j], recv_sem=c_recv.at[frm * slots + j],
            device_id=peer(line, to), device_id_type=MESH)

    def fill(dst, src, first):
        for i in range(cap):
            dst[i * bands:(i + 1) * bands, :] = src[source_row[first + i]]

    copy_val.wait()
    copy_cond.wait()

    def pack_step(step, carry):
        j = slot_at(step)

        def pack_to(d, carry):
            to = lax.rem(place + d, inner)
            first = (to * slots + j) * cap
            fill(pack_v.at[to, j], val_in, first)
            v_copy(j, to, place).start()
            fill(pack_c.at[to, j], cond_in, first)
            c_copy(j, to, place).start()
            return carry

        lax.fori_loop(1, inner, pack_to, 0)
        first = (place * slots + j) * cap
        fill(vbuf.at[core, j, place], val_in, first)
        fill(cbuf.at[j, place], cond_in, first)
        return carry

    lax.fori_loop(0, slots, pack_step, 0)

    def w_event(t, l):
        below, above = line - t, line + t

        @pl.when(below >= 0)
        def _():
            w_copy(below * local + l, line, w_up).wait_recv()

            @pl.when(line < outer - 1)
            def _():
                w_copy(below * local + l, line + 1, w_up).start()

        @pl.when(above < outer)
        def _():
            w_copy(above * local + l, line, w_down).wait_recv()

            @pl.when(line > 0)
            def _():
                w_copy(above * local + l, line - 1, w_down).start()

    def s_copy(j):
        return pltpu.make_async_remote_copy(
            src_ref=vbuf.at[core, j], dst_ref=vbuf.at[core, j], send_sem=s_send.at[j],
            recv_sem=s_recv.at[j], device_id=sibling, device_id_type=MESH)

    def s_arrived(j):
        return pltpu.make_async_remote_copy(
            src_ref=vbuf.at[1 - core, j], dst_ref=vbuf.at[1 - core, j], send_sem=s_send.at[j],
            recv_sem=s_recv.at[j], device_id=sibling, device_id_type=MESH)

    nt = (((1,), (1,)), ((), ()))
    width = app.shape[1]
    g_all = app.shape[2]
    g_tile = min(256, g_all)
    row_pair = lax.broadcasted_iota(jnp.int32, (rows, width), 0) // bands
    col_pair = lax.broadcasted_iota(jnp.int32, (rows, width), 1) // bands
    same_pair = row_pair == col_pair
    own_lane = (lax.broadcasted_iota(jnp.int32, (cap, bands // 2, 128), 1)
                == lax.broadcasted_iota(jnp.int32, (cap, bands // 2, 128), 2) // bands)

    def compute(j):
        def apply_tile(gt, carry):
            cols = pl.ds(pl.multiple_of(gt * g_tile, g_tile), g_tile)
            total = jnp.zeros((inner * rows, g_tile), jnp.float32)
            for h in range(2):
                total = total + lax.dot_general(
                    vbuf[h, j].reshape(inner * rows, half),
                    wbuf[j, cols, h * half:(h + 1) * half], nt,
                    preferred_element_type=jnp.float32)
            app[:, 0:rows, cols] = total.astype(jnp.bfloat16).reshape(inner, rows, g_tile)
            return carry

        lax.fori_loop(0, g_all // g_tile, apply_tile, 0)

        def contract(s, carry):
            prod = lax.dot_general(cbuf[j, s], app[s], nt, preferred_element_type=jnp.float32)
            prod = jnp.where(same_pair, prod, 0.0)
            folded = prod[:, 0:128]
            for x in range(1, width // 128):
                folded = folded + prod[:, x * 128:(x + 1) * 128]
            shift = 64
            while shift >= bands:
                folded = folded + pltpu.roll(folded, shift, 1)
                shift //= 2
            folded = folded.reshape(cap, bands, 128)
            for h in range(2):
                piece = folded[:, h * (bands // 2):(h + 1) * (bands // 2), :]
                piece = jnp.sum(jnp.where(own_lane, piece, 0.0), axis=1)
                if cap_pad > cap:
                    piece = jnp.concatenate(
                        [piece, jnp.zeros((cap_pad - cap, 128), jnp.float32)], axis=0)
                part[h, s, j] = piece
            return carry

        lax.fori_loop(0, inner, contract, 0)

    events = {}
    count = (outer - 1) * local
    for e in range(count):
        events[min(slots - 1, (e + 1) * slots // count)] = (1 + e // local, e % local)

    def work(step, carry):
        for k, (t, l) in events.items():
            @pl.when(step == k)
            def _():
                w_event(t, l)

        @pl.when(step < slots)
        def _():
            j = slot_at(step)

            def take(d, carry):
                frm = lax.rem(place + d, inner)
                v_copy(j, frm, frm).wait_recv()
                return carry

            lax.fori_loop(1, inner, take, 0)
            s_copy(j).start()

        @pl.when(step > 0)
        def _():
            j = slot_at(step - 1)
            s_arrived(j).wait_recv()

            def take(d, carry):
                frm = lax.rem(place + d, inner)
                c_copy(j, frm, frm).wait_recv()
                return carry

            lax.fori_loop(1, inner, take, 0)
            compute(j)

        return carry

    lax.fori_loop(0, slots + 1, work, 0)

    p_copy = pltpu.make_async_remote_copy(
        src_ref=part.at[1 - core], dst_ref=sib, send_sem=p_sem.at[0], recv_sem=p_sem.at[1],
        device_id=sibling, device_id_type=MESH)
    p_copy.start()
    p_copy.wait_recv()

    def r_copy(to, frm):
        return pltpu.make_async_remote_copy(
            src_ref=back.at[to], dst_ref=ret.at[frm], send_sem=r_send.at[to],
            recv_sem=r_recv.at[frm], device_id=peer(line, to), device_id_type=MESH)

    def give(d, carry):
        to = lax.rem(place + d, inner)
        back[to] = (part[core, to] + sib[to]).reshape(back.shape[1:])
        r_copy(to, place).start()
        return carry

    lax.fori_loop(1, inner, give, 0)
    ret[place] = (part[core, place] + sib[place]).reshape(ret.shape[1:])

    def settle(j, carry):
        def sent(d, carry):
            to = lax.rem(place + d, inner)
            v_copy(j, to, place).wait_send()
            c_copy(j, to, place).wait_send()
            return carry

        lax.fori_loop(1, inner, sent, 0)
        s_copy(j).wait_send()

        @pl.when((line < outer - 1) & (j // local <= line))
        def _():
            w_copy(j, line + 1, w_up).wait_send()

        @pl.when((line > 0) & (j // local >= line))
        def _():
            w_copy(j, line - 1, w_down).wait_send()

        return carry

    lax.fori_loop(0, slots, settle, 0)
    p_copy.wait_send()

    def got(d, carry):
        other = lax.rem(place + d, inner)
        r_copy(other, other).wait_recv()
        r_copy(other, place).wait_send()
        return carry

    lax.fori_loop(1, inner, got, 0)

    flat = ret.reshape(ret.shape[0] * ret.shape[1], ret.shape[2])

    def place_rows(b, carry):
        for i in range(8):
            row = b * 8 + i
            out_ref[pl.ds(row, 1), :] = flat[pl.ds(target[row], 1), :]
        return carry

    lax.fori_loop(0, out_ref.shape[0] // 8, place_rows, 0)


def visit_order(outer, local):
    steps = []
    for z in range(outer):
        order = [z * local + l for l in range(local)]
        for t in range(1, outer):
            for l in range(local):
                order += [y * local + l for y in (z - t, z + t) if 0 <= y < outer]
        steps.append(order)
    return steps


def body(peer_count, q_of_pair, q_slot, valence, conduction, screened):
    pair_count, bands, half = valence.shape
    local, g_rows, g_cols = screened.shape
    q_total = q_slot.shape[0]
    cap = max(2, (3 * pair_count + 2 * q_total - 1) // (2 * q_total))
    cap_pad = -(-cap // 8) * 8
    outer = 4 if peer_count % 4 == 0 else 1
    inner = peer_count // outer
    slots = outer * local
    rows = cap * bands
    width = -(-rows // 128) * 128

    q_ids = q_of_pair[:, 0]
    q_match = q_ids[:, None] == jnp.arange(q_total, dtype=jnp.int32)[None, :]
    slot_index = jnp.sum(jnp.where(q_match, q_slot[None, :], 0), axis=1)
    order_row = jnp.arange(pair_count, dtype=jnp.int32)
    same_q = (q_ids[:, None] == q_ids[None, :]) & (order_row[None, :] < order_row[:, None])
    rank = jnp.sum(same_q.astype(jnp.int32), axis=1)
    owner = slot_index // local
    group = owner % inner * slots + owner // inner * local + slot_index % local
    packed = group * cap + rank
    target = group * cap_pad + rank
    hit = packed[None, :] == jnp.arange(inner * slots * cap, dtype=jnp.int32)[:, None]
    source_row = jnp.sum(jnp.where(hit, order_row[None, :], 0), axis=1)

    smem = pl.BlockSpec(memory_space=pltpu.SMEM)
    anywhere = pl.BlockSpec(memory_space=pl.ANY)
    dma = pltpu.SemaphoreType.DMA
    bf16, f32 = jnp.bfloat16, jnp.float32
    return pl.pallas_call(
        functools.partial(kernel, outer, inner, local, cap, cap_pad, visit_order(outer, local)),
        out_shape=jax.ShapeDtypeStruct((pair_count, bands * bands // 2), f32),
        in_specs=[smem, smem, anywhere, anywhere, anywhere],
        out_specs=pl.BlockSpec(memory_space=pltpu.VMEM),
        scratch_shapes=[
            pltpu.VMEM((pair_count, bands, half), bf16),
            pltpu.VMEM((pair_count, bands, half), bf16),
            pltpu.VMEM((inner, slots, rows, half), bf16),
            pltpu.VMEM((inner, slots, rows, half), bf16),
            pltpu.VMEM((2, slots, inner, rows, half), bf16),
            pltpu.VMEM((slots, inner, rows, half), bf16),
            pltpu.VMEM((slots, g_rows, g_cols), bf16),
            pltpu.VMEM((inner, width, g_rows), bf16),
            pltpu.VMEM((2, inner, slots, cap_pad, 128), f32),
            pltpu.VMEM((inner, slots, cap_pad, 128), f32),
            pltpu.VMEM((inner, slots * cap_pad, 128), f32),
            pltpu.VMEM((inner, slots * cap_pad, 128), f32),
            dma((3,)), dma((slots,)), dma((slots,)), dma((slots,)),
            dma((inner * slots,)), dma((inner * slots,)),
            dma((inner * slots,)), dma((inner * slots,)),
            dma((slots,)), dma((slots,)), dma((2,)), dma((inner,)), dma((inner,)),
        ],
        compiler_params=pltpu.CompilerParams(
            collective_id=0, has_side_effects=True, vmem_limit_bytes=58 * 1024 * 1024),
        cost_estimate=pl.CostEstimate(
            flops=2 * inner * slots * rows * g_rows * g_cols, transcendentals=0,
            bytes_accessed=4 * pair_count * bands * half + 2 * local * g_rows * g_cols),
    )(source_row, target, valence, conduction, screened)


def solution(mesh):
    in_specs = (P("pb", None), P(), P("pb", None, "ga"), P("pb", None, "ga"), P("pb", "ga", None))
    return jax.shard_map(functools.partial(body, mesh.shape["pb"]), mesh=mesh, in_specs=in_specs,
                         out_specs=P("pb", "ga"), check_vma=False)
```

time: 380 us -> 160 us (0.42)
  blocking collectives: 289 us -> 0 us
  Pallas kernels: 0 us -> 156 us
  waiting for transfers between devices: 26 us -> 0 us
  local copies, waits for them, and re-layouts: 17.5 us -> 1.57 us
  matrix products: 14.2 us -> 0 us
  between operations: 13.5 us -> 0.01 us
  other arithmetic: 12.2 us -> 3.05 us
  starting transfers between devices: 6.83 us -> 0 us
    all_to_all x2 -> x0, blocking collectives: 289 us -> none  [the longest x1 147 us: body(): lax.all_to_all(pack_rows(valence), 'pb', split_axis=0, concat_axis=0, til...]
    pallas_call x0 -> x1, Pallas kernels: none -> 156 us  [body(): pl.pallas_call(functools.partial(kernel, outer, inner, local, cap, cap_pa...]
    psum x1 -> x0, waiting for transfers between devices: 16.9 us -> none  [body(): summed = lax.psum(partial_value, 'ga')]
    dot_general x1 -> x0, matrix products: 14.2 us -> none  [body(): jnp.einsum('placg,plabg->placb', cond_recv, applied, preferred_element_ty...]
    gather x3 -> x0, local copies, waits for them, and re-layouts: 12.4 us -> none  [the longest x2 11.7 us: pack_rows(): rows = jnp.take(values, source_row, axis=0)]
    select_n x4 -> x0, other arithmetic: 10.1 us -> none  [the longest x1 9.32 us: pack_rows(): rows = jnp.where(filled[:, None, None], rows, jnp.zeros_like(rows))]
    all_to_all x1 -> x0, waiting for transfers between devices: 9.06 us -> none  [body(): lax.all_to_all(my_share, 'pb', split_axis=0, concat_axis=0, tiled=True)]
    all_to_all x1 -> x0, starting transfers between devices: 6.79 us -> none  [body(): lax.all_to_all(my_share, 'pb', split_axis=0, concat_axis=0, tiled=True)]
  transfers between devices with their start and end apart: 3 -> 0, of which waited for: 2 -> 0; matrix products, arithmetic and copies ran while one was open for 0% -> 0% of each run, Pallas kernels for 0% -> 0%
where the time goes in v1:
time: 160 us
  Pallas kernels  156 us (98%)
  other arithmetic  3.05 us (2%)
    pallas_call x1, Pallas kernels, body(): pl.pallas_call(functools.partial(kernel, outer, inner, local, cap, cap_pa...  156 us

profile of v1, /device:TPU:0, one launch (start us, length us, event | category | flops | bytes accessed | tf_op | source)
XLA Modules:
  0.0 160.2 jit_solution(16534093347358164612)
XLA Ops:
  0.0 0.9 convert_reduce_fusion
  0.9 0.8 select_reduce_fusion.1
  1.7 0.6 multiply_add_fusion
  2.3 0.7 select_reduce_fusion.source_row
  3.1 155.5 %shard_map.55 = f32[256,128]{1,0:T(8,128)} custom-call(s32[384]{0:T(512)} %select_reduce_fusion.source_row, s32[256]{0:T(256)} %get-tuple-element.5.target, bf16[256,16,512]{2,1,0:T(8,128)(2,1)} %val_hbm.1, bf16[256,16,512]{2,1,0:T(8,128)(2,1)} %cond_hbm.1, bf16[2,512,1024]{2,1,0:T(8,128)(2,1)} %w_hbm.1), custom_call_target="tpu_custom_call" | custom-call | flops 6442450944 | bytes 10485760 | tf_op jit(solution)/shard_map/pallas_call | solution.py:333
  158.6 1.6 copy.7
  (1 shorter events, 0.0 us)

commit v2 on v1

--- a/solution.py
+++ b/solution.py
@@ -8,13 +8,14 @@
 from jax.sharding import PartitionSpec as P
 
 MESH = pl.DeviceIdType.MESH
+WINDOW = 3
 
 
 def kernel(outer, inner, local, cap, cap_pad, steps,
            source_row, target, val_hbm, cond_hbm, w_hbm, out_ref,
            val_in, cond_in, pack_v, pack_c, vbuf, cbuf, wbuf, app, part, sib, back, ret,
            in_sem, w_up, w_down, w_recv, v_send, c_send, v_recv, c_recv,
-           s_send, s_recv, p_sem, r_send, r_recv):
+           s_send, s_recv, p_send, p_recv, r_send, r_recv):
     me = lax.axis_index("pb")
     core = lax.axis_index("ga")
     line, place = me // inner, lax.rem(me, inner)
@@ -52,11 +53,10 @@
     copy_val = pltpu.make_async_copy(val_hbm, val_in, in_sem.at[0])
     copy_cond = pltpu.make_async_copy(cond_hbm, cond_in, in_sem.at[1])
     copy_w = pltpu.make_async_copy(w_hbm, wbuf.at[pl.ds(line * local, local)], in_sem.at[2])
-    copy_w.start()
     copy_val.start()
     copy_cond.start()
+    copy_w.start()
     app[...] = jnp.zeros_like(app)
-    copy_w.wait()
     pl.semaphore_wait(barrier, inner + (line > 0).astype(jnp.int32)
                       + (line < outer - 1).astype(jnp.int32))
 
@@ -65,14 +65,22 @@
             src_ref=wbuf.at[j], dst_ref=wbuf.at[j], send_sem=send.at[j],
             recv_sem=w_recv.at[j], device_id=peer(to_line, place), device_id_type=MESH)
 
-    for l in range(local):
+    def send_own(l):
+        def own_copy(to_line, send):
+            return pltpu.make_async_remote_copy(
+                src_ref=w_hbm.at[l], dst_ref=wbuf.at[line * local + l],
+                send_sem=send.at[line * local + l], recv_sem=w_recv.at[line * local + l],
+                device_id=peer(to_line, place), device_id_type=MESH)
+
         @pl.when(line < outer - 1)
         def _():
-            w_copy(line * local + l, line + 1, w_up).start()
+            own_copy(line + 1, w_up).start()
 
         @pl.when(line > 0)
         def _():
-            w_copy(line * local + l, line - 1, w_down).start()
+            own_copy(line - 1, w_down).start()
+
+    send_own(0)
 
     def v_copy(j, to, frm):
         return pltpu.make_async_remote_copy(
@@ -111,7 +119,8 @@
         fill(cbuf.at[j, place], cond_in, first)
         return carry
 
-    lax.fori_loop(0, slots, pack_step, 0)
+    lax.fori_loop(0, WINDOW, pack_step, 0)
+    copy_w.wait()
 
     def w_event(t, l):
         below, above = line - t, line + t
@@ -183,7 +192,7 @@
                 if cap_pad > cap:
                     piece = jnp.concatenate(
                         [piece, jnp.zeros((cap_pad - cap, 128), jnp.float32)], axis=0)
-                part[h, s, j] = piece
+                part[h, j, s] = piece
             return carry
 
         lax.fori_loop(0, inner, contract, 0)
@@ -191,27 +200,60 @@
     events = {}
     count = (outer - 1) * local
     for e in range(count):
-        events[min(slots - 1, (e + 1) * slots // count)] = (1 + e // local, e % local)
+        events[1 + e * (slots + 1) // count] = (1 + e // local, e % local)
+
+    def p_copy(j):
+        return pltpu.make_async_remote_copy(
+            src_ref=part.at[1 - core, j], dst_ref=sib.at[j], send_sem=p_send.at[j],
+            recv_sem=p_recv.at[j], device_id=sibling, device_id_type=MESH)
+
+    def r_copy(j, to, frm):
+        return pltpu.make_async_remote_copy(
+            src_ref=back.at[to, j], dst_ref=ret.at[frm, j], send_sem=r_send.at[to * slots + j],
+            recv_sem=r_recv.at[frm * slots + j], device_id=peer(line, to), device_id_type=MESH)
 
     def work(step, carry):
+        @pl.when(step < slots)
+        def _():
+            j = slot_at(step)
+
+            def take(d, carry):
+                frm = lax.rem(place + d, inner)
+                v_copy(j, frm, frm).wait_recv()
+                return carry
+
+            lax.fori_loop(1, inner, take, 0)
+            s_copy(j).start()
+
+        for l in range(1, local):
+            @pl.when(step == l - 1)
+            def _():
+                send_own(l)
+
+        @pl.when(step + WINDOW < slots)
+        def _():
+            pack_step(step + WINDOW, 0)
+
         for k, (t, l) in events.items():
             @pl.when(step == k)
             def _():
                 w_event(t, l)
 
-        @pl.when(step < slots)
-        def _():
-            j = slot_at(step)
-
-            def take(d, carry):
-                frm = lax.rem(place + d, inner)
-                v_copy(j, frm, frm).wait_recv()
+        @pl.when(step > 1)
+        def _():
+            j = slot_at(step - 2)
+            p_copy(j).wait_recv()
+
+            def give(d, carry):
+                to = lax.rem(place + d, inner)
+                back[to, j] = part[core, j, to] + sib[j, to]
+                r_copy(j, to, place).start()
                 return carry
 
-            lax.fori_loop(1, inner, take, 0)
-            s_copy(j).start()
-
-        @pl.when(step > 0)
+            lax.fori_loop(1, inner, give, 0)
+            ret[place, j] = part[core, j, place] + sib[j, place]
+
+        @pl.when((step > 0) & (step <= slots))
         def _():
             j = slot_at(step - 1)
             s_arrived(j).wait_recv()
@@ -223,30 +265,11 @@
 
             lax.fori_loop(1, inner, take, 0)
             compute(j)
+            p_copy(j).start()
 
         return carry
 
-    lax.fori_loop(0, slots + 1, work, 0)
-
-    p_copy = pltpu.make_async_remote_copy(
-        src_ref=part.at[1 - core], dst_ref=sib, send_sem=p_sem.at[0], recv_sem=p_sem.at[1],
-        device_id=sibling, device_id_type=MESH)
-    p_copy.start()
-    p_copy.wait_recv()
-
-    def r_copy(to, frm):
-        return pltpu.make_async_remote_copy(
-            src_ref=back.at[to], dst_ref=ret.at[frm], send_sem=r_send.at[to],
-            recv_sem=r_recv.at[frm], device_id=peer(line, to), device_id_type=MESH)
-
-    def give(d, carry):
-        to = lax.rem(place + d, inner)
-        back[to] = (part[core, to] + sib[to]).reshape(back.shape[1:])
-        r_copy(to, place).start()
-        return carry
-
-    lax.fori_loop(1, inner, give, 0)
-    ret[place] = (part[core, place] + sib[place]).reshape(ret.shape[1:])
+    lax.fori_loop(0, slots + 2, work, 0)
 
     def settle(j, carry):
         def sent(d, carry):
@@ -257,6 +280,7 @@
 
         lax.fori_loop(1, inner, sent, 0)
         s_copy(j).wait_send()
+        p_copy(j).wait_send()
 
         @pl.when((line < outer - 1) & (j // local <= line))
         def _():
@@ -269,17 +293,19 @@
         return carry
 
     lax.fori_loop(0, slots, settle, 0)
-    p_copy.wait_send()
-
-    def got(d, carry):
-        other = lax.rem(place + d, inner)
-        r_copy(other, other).wait_recv()
-        r_copy(other, place).wait_send()
-        return carry
-
-    lax.fori_loop(1, inner, got, 0)
-
-    flat = ret.reshape(ret.shape[0] * ret.shape[1], ret.shape[2])
+
+    def got(j, carry):
+        def each(d, carry):
+            other = lax.rem(place + d, inner)
+            r_copy(j, other, other).wait_recv()
+            r_copy(j, other, place).wait_send()
+            return carry
+
+        return lax.fori_loop(1, inner, each, carry)
+
+    lax.fori_loop(0, slots, got, 0)
+
+    flat = ret.reshape(inner * slots * cap_pad, 128)
 
     def place_rows(b, carry):
         for i in range(8):
@@ -344,14 +370,15 @@
             pltpu.VMEM((slots, inner, rows, half), bf16),
             pltpu.VMEM((slots, g_rows, g_cols), bf16),
             pltpu.VMEM((inner, width, g_rows), bf16),
-            pltpu.VMEM((2, inner, slots, cap_pad, 128), f32),
+            pltpu.VMEM((2, slots, inner, cap_pad, 128), f32),
+            pltpu.VMEM((slots, inner, cap_pad, 128), f32),
             pltpu.VMEM((inner, slots, cap_pad, 128), f32),
-            pltpu.VMEM((inner, slots * cap_pad, 128), f32),
-            pltpu.VMEM((inner, slots * cap_pad, 128), f32),
+            pltpu.VMEM((inner, slots, cap_pad, 128), f32),
             dma((3,)), dma((slots,)), dma((slots,)), dma((slots,)),
             dma((inner * slots,)), dma((inner * slots,)),
             dma((inner * slots,)), dma((inner * slots,)),
-            dma((slots,)), dma((slots,)), dma((2,)), dma((inner,)), dma((inner,)),
+            dma((slots,)), dma((slots,)), dma((slots,)), dma((slots,)),
+            dma((inner * slots,)), dma((inner * slots,)),
         ],
         compiler_params=pltpu.CompilerParams(
             collective_id=0, has_side_effects=True, vmem_limit_bytes=58 * 1024 * 1024),

time: 160 us -> 160 us (level)
  no operation moved by 1% of the time
where the time goes in v2:
time: 160 us
  Pallas kernels  155 us (97%)
  other arithmetic  3.05 us (2%)
    pallas_call x1, Pallas kernels, body(): pl.pallas_call(functools.partial(kernel, outer, inner, local, cap, cap_pa...  155 us

profile of v2, /device:TPU:0, one launch (start us, length us, event | category | flops | bytes accessed | tf_op | source)
XLA Modules:
  0.0 159.7 jit_solution(14786161008605860953)
XLA Ops:
  0.0 0.9 convert_reduce_fusion
  0.9 0.8 select_reduce_fusion.1
  1.7 0.6 multiply_add_fusion
  2.3 0.7 select_reduce_fusion.source_row
  3.1 155.1 %shard_map.55 = f32[256,128]{1,0:T(8,128)} custom-call(s32[384]{0:T(512)} %select_reduce_fusion.source_row, s32[256]{0:T(256)} %get-tuple-element.5.target, bf16[256,16,512]{2,1,0:T(8,128)(2,1)} %val_hbm.1, bf16[256,16,512]{2,1,0:T(8,128)(2,1)} %cond_hbm.1, bf16[2,512,1024]{2,1,0:T(8,128)(2,1)} %w_hbm.1), custom_call_target="tpu_custom_call" | custom-call | flops 6442450944 | bytes 10485760 | tf_op jit(solution)/shard_map/pallas_call | solution.py:359
  158.2 1.6 copy.7
  (1 shorter events, 0.0 us)

commit v3 on v2

--- a/solution.py
+++ b/solution.py
@@ -54,8 +54,6 @@
     copy_cond = pltpu.make_async_copy(cond_hbm, cond_in, in_sem.at[1])
     copy_w = pltpu.make_async_copy(w_hbm, wbuf.at[pl.ds(line * local, local)], in_sem.at[2])
     copy_val.start()
-    copy_cond.start()
-    copy_w.start()
     app[...] = jnp.zeros_like(app)
     pl.semaphore_wait(barrier, inner + (line > 0).astype(jnp.int32)
                       + (line < outer - 1).astype(jnp.int32))
@@ -98,28 +96,39 @@
         for i in range(cap):
             dst[i * bands:(i + 1) * bands, :] = src[source_row[first + i]]
 
-    copy_val.wait()
-    copy_cond.wait()
+    def pack_val(j):
+        def pack_to(d, carry):
+            to = lax.rem(place + d, inner)
+            fill(pack_v.at[to, j], val_in, (to * slots + j) * cap)
+            v_copy(j, to, place).start()
+            return carry
+
+        lax.fori_loop(1, inner, pack_to, 0)
+        fill(vbuf.at[core, j, place], val_in, (place * slots + j) * cap)
+
+    def pack_cond(j):
+        def pack_to(d, carry):
+            to = lax.rem(place + d, inner)
+            fill(pack_c.at[to, j], cond_in, (to * slots + j) * cap)
+            c_copy(j, to, place).start()
+            return carry
+
+        lax.fori_loop(1, inner, pack_to, 0)
+        fill(cbuf.at[j, place], cond_in, (place * slots + j) * cap)
 
     def pack_step(step, carry):
         j = slot_at(step)
-
-        def pack_to(d, carry):
-            to = lax.rem(place + d, inner)
-            first = (to * slots + j) * cap
-            fill(pack_v.at[to, j], val_in, first)
-            v_copy(j, to, place).start()
-            fill(pack_c.at[to, j], cond_in, first)
-            c_copy(j, to, place).start()
-            return carry
-
-        lax.fori_loop(1, inner, pack_to, 0)
-        first = (place * slots + j) * cap
-        fill(vbuf.at[core, j, place], val_in, first)
-        fill(cbuf.at[j, place], cond_in, first)
+        pack_val(j)
+        pack_cond(j)
         return carry
 
-    lax.fori_loop(0, WINDOW, pack_step, 0)
+    copy_val.wait()
+    copy_cond.start()
+    copy_w.start()
+    pack_val(slot_at(0))
+    copy_cond.wait()
+    pack_cond(slot_at(0))
+    lax.fori_loop(1, WINDOW, pack_step, 0)
     copy_w.wait()
 
     def w_event(t, l):
@@ -174,6 +183,13 @@
             return carry
 
         lax.fori_loop(0, g_all // g_tile, apply_tile, 0)
+
+        def take(d, carry):
+            frm = lax.rem(place + d, inner)
+            c_copy(j, frm, frm).wait_recv()
+            return carry
+
+        lax.fori_loop(1, inner, take, 0)
 
         def contract(s, carry):
             prod = lax.dot_general(cbuf[j, s], app[s], nt, preferred_element_type=jnp.float32)
@@ -258,12 +274,6 @@
             j = slot_at(step - 1)
             s_arrived(j).wait_recv()
 
-            def take(d, carry):
-                frm = lax.rem(place + d, inner)
-                c_copy(j, frm, frm).wait_recv()
-                return carry
-
-            lax.fori_loop(1, inner, take, 0)
             compute(j)
             p_copy(j).start()
 

time: 160 us -> 157 us (0.981)
  Pallas kernels: 155 us -> 152 us
    pallas_call x1, Pallas kernels: 155 us -> 152 us  [body(): pl.pallas_call(functools.partial(kernel, outer, inner, local, cap, cap_pa...]
where the time goes in v3:
time: 157 us
  Pallas kernels  152 us (97%)
  other arithmetic  3.05 us (2%)
  local copies, waits for them, and re-layouts  1.57 us (1%)
    pallas_call x1, Pallas kernels, body(): pl.pallas_call(functools.partial(kernel, outer, inner, local, cap, cap_pa...  152 us

profile of v3, /device:TPU:0, one launch (start us, length us, event | category | flops | bytes accessed | tf_op | source)
XLA Modules:
  0.0 156.7 jit_solution(7906472918437425404)
XLA Ops:
  0.0 0.9 convert_reduce_fusion
  0.9 0.8 select_reduce_fusion.1
  1.7 0.6 multiply_add_fusion
  2.3 0.7 select_reduce_fusion.source_row
  3.1 152.0 %shard_map.55 = f32[256,128]{1,0:T(8,128)} custom-call(s32[384]{0:T(512)} %select_reduce_fusion.source_row, s32[256]{0:T(256)} %get-tuple-element.5.target, bf16[256,16,512]{2,1,0:T(8,128)(2,1)} %val_hbm.1, bf16[256,16,512]{2,1,0:T(8,128)(2,1)} %cond_hbm.1, bf16[2,512,1024]{2,1,0:T(8,128)(2,1)} %w_hbm.1), custom_call_target="tpu_custom_call" | custom-call | flops 6442450944 | bytes 10485760 | tf_op jit(solution)/shard_map/pallas_call | solution.py:369
  155.1 1.6 %copy.7 = f32[256,128]{1,0:T(8,128)} copy(f32[256,128]{1,0:T(8,128)} %shard_map.55) | data formatting | bytes 262144
  (1 shorter events, 0.0 us)

commit v4 on v3

--- a/solution.py
+++ b/solution.py
@@ -8,14 +8,14 @@
 from jax.sharding import PartitionSpec as P
 
 MESH = pl.DeviceIdType.MESH
-WINDOW = 3
+WINDOW = 4
 
 
 def kernel(outer, inner, local, cap, cap_pad, steps,
            source_row, target, val_hbm, cond_hbm, w_hbm, out_ref,
-           val_in, cond_in, pack_v, pack_c, vbuf, cbuf, wbuf, app, part, sib, back, ret,
+           val_in, cond_in, pack_v, pack_c, vbuf, cbuf, wbuf, hop_v, hop_c, app, part, sib, back, ret,
            in_sem, w_up, w_down, w_recv, v_send, c_send, v_recv, c_recv,
-           s_send, s_recv, p_send, p_recv, r_send, r_recv):
+           s_send, s_recv, p_send, p_recv, r_send, r_recv, hop_send, hop_recv):
     me = lax.axis_index("pb")
     core = lax.axis_index("ga")
     line, place = me // inner, lax.rem(me, inner)
@@ -96,7 +96,51 @@
         for i in range(cap):
             dst[i * bands:(i + 1) * bands, :] = src[source_row[first + i]]
 
+    relay = inner == 4
+    across_x = place + 1 - 2 * lax.rem(place, 2)
+    across_y = place + 2 - 4 * (place // 2)
+    diagonal = inner - 1 - place
+
+    def v_first(j):
+        return pltpu.make_async_remote_copy(
+            src_ref=pack_v.at[diagonal, j], dst_ref=hop_v.at[j],
+            send_sem=v_send.at[diagonal * slots + j], recv_sem=hop_recv.at[j],
+            device_id=peer(line, across_x), device_id_type=MESH)
+
+    def c_first(j):
+        return pltpu.make_async_remote_copy(
+            src_ref=pack_c.at[diagonal, j], dst_ref=hop_c.at[j],
+            send_sem=c_send.at[diagonal * slots + j], recv_sem=hop_recv.at[slots + j],
+            device_id=peer(line, across_y), device_id_type=MESH)
+
+    def v_second(j):
+        return pltpu.make_async_remote_copy(
+            src_ref=hop_v.at[j], dst_ref=vbuf.at[core, j, across_x],
+            send_sem=hop_send.at[j], recv_sem=v_recv.at[across_x * slots + j],
+            device_id=peer(line, across_y), device_id_type=MESH)
+
+    def c_second(j):
+        return pltpu.make_async_remote_copy(
+            src_ref=hop_c.at[j], dst_ref=cbuf.at[j, across_y],
+            send_sem=hop_send.at[slots + j], recv_sem=c_recv.at[across_y * slots + j],
+            device_id=peer(line, across_x), device_id_type=MESH)
+
+    def hand_on(j):
+        v_first(j).wait_recv()
+        v_second(j).start()
+        c_first(j).wait_recv()
+        c_second(j).start()
+
     def pack_val(j):
+        if relay:
+            fill(pack_v.at[diagonal, j], val_in, (diagonal * slots + j) * cap)
+            v_first(j).start()
+            for to in (across_x, across_y):
+                fill(pack_v.at[to, j], val_in, (to * slots + j) * cap)
+                v_copy(j, to, place).start()
+            fill(vbuf.at[core, j, place], val_in, (place * slots + j) * cap)
+            return
+
         def pack_to(d, carry):
             to = lax.rem(place + d, inner)
             fill(pack_v.at[to, j], val_in, (to * slots + j) * cap)
@@ -107,6 +151,15 @@
         fill(vbuf.at[core, j, place], val_in, (place * slots + j) * cap)
 
     def pack_cond(j):
+        if relay:
+            fill(pack_c.at[diagonal, j], cond_in, (diagonal * slots + j) * cap)
+            c_first(j).start()
+            for to in (across_x, across_y):
+                fill(pack_c.at[to, j], cond_in, (to * slots + j) * cap)
+                c_copy(j, to, place).start()
+            fill(cbuf.at[j, place], cond_in, (place * slots + j) * cap)
+            return
+
         def pack_to(d, carry):
             to = lax.rem(place + d, inner)
             fill(pack_c.at[to, j], cond_in, (to * slots + j) * cap)
@@ -229,6 +282,11 @@
             recv_sem=r_recv.at[frm * slots + j], device_id=peer(line, to), device_id_type=MESH)
 
     def work(step, carry):
+        if relay:
+            @pl.when(step + 1 < slots)
+            def _():
+                hand_on(slot_at(step + 1))
+
         @pl.when(step < slots)
         def _():
             j = slot_at(step)
@@ -279,6 +337,8 @@
 
         return carry
 
+    if relay:
+        hand_on(slot_at(0))
     lax.fori_loop(0, slots + 2, work, 0)
 
     def settle(j, carry):
@@ -289,6 +349,9 @@
             return carry
 
         lax.fori_loop(1, inner, sent, 0)
+        if relay:
+            v_second(j).wait_send()
+            c_second(j).wait_send()
         s_copy(j).wait_send()
         p_copy(j).wait_send()
 
@@ -379,6 +442,8 @@
             pltpu.VMEM((2, slots, inner, rows, half), bf16),
             pltpu.VMEM((slots, inner, rows, half), bf16),
             pltpu.VMEM((slots, g_rows, g_cols), bf16),
+            pltpu.VMEM((slots, rows, half), bf16),
+            pltpu.VMEM((slots, rows, half), bf16),
             pltpu.VMEM((inner, width, g_rows), bf16),
             pltpu.VMEM((2, slots, inner, cap_pad, 128), f32),
             pltpu.VMEM((slots, inner, cap_pad, 128), f32),
@@ -389,6 +454,7 @@
             dma((inner * slots,)), dma((inner * slots,)),
             dma((slots,)), dma((slots,)), dma((slots,)), dma((slots,)),
             dma((inner * slots,)), dma((inner * slots,)),
+            dma((2 * slots,)), dma((2 * slots,)),
         ],
         compiler_params=pltpu.CompilerParams(
             collective_id=0, has_side_effects=True, vmem_limit_bytes=58 * 1024 * 1024),

time: 157 us -> 191 us (1.22)
  Pallas kernels: 152 us -> 186 us
    pallas_call x1, Pallas kernels: 152 us -> 186 us  [body(): pl.pallas_call(functools.partial(kernel, outer, inner, local, cap, cap_pa...]
where the time goes in v4:
time: 191 us; the launch traced here: 190 us
  Pallas kernels  186 us (97%)
  other arithmetic  3.05 us (2%)
    pallas_call x1, Pallas kernels, body(): pl.pallas_call(functools.partial(kernel, outer, inner, local, cap, cap_pa...  186 us

profile of v4, /device:TPU:0, one launch (start us, length us, event | category | flops | bytes accessed | tf_op | source)
XLA Modules:
  0.0 190.4 jit_solution(15568430942749178717)
XLA Ops:
  0.0 0.9 convert_reduce_fusion
  0.9 0.8 select_reduce_fusion.1
  1.7 0.6 multiply_add_fusion
  2.3 0.7 select_reduce_fusion.source_row
  3.1 185.8 %shard_map.55 = f32[256,128]{1,0:T(8,128)} custom-call(s32[384]{0:T(512)} %select_reduce_fusion.source_row, s32[256]{0:T(256)} %get-tuple-element.5.target, bf16[256,16,512]{2,1,0:T(8,128)(2,1)} %val_hbm.1, bf16[256,16,512]{2,1,0:T(8,128)(2,1)} %cond_hbm.1, bf16[2,512,1024]{2,1,0:T(8,128)(2,1)} %w_hbm.1), custom_call_target="tpu_custom_call" | custom-call | flops 6442450944 | bytes 10485760 | tf_op jit(solution)/shard_map/pallas_call | solution.py:432
  188.9 1.6 copy.7
  (1 shorter events, 0.0 us)

commit v5 on v3

--- a/solution.py
+++ b/solution.py
@@ -78,7 +78,8 @@
         def _():
             own_copy(line - 1, w_down).start()
 
-    send_own(0)
+    for l in range(local):
+        send_own(l)
 
     def v_copy(j, to, frm):
         return pltpu.make_async_remote_copy(
@@ -184,14 +185,13 @@
 
         lax.fori_loop(0, g_all // g_tile, apply_tile, 0)
 
-        def take(d, carry):
-            frm = lax.rem(place + d, inner)
-            c_copy(j, frm, frm).wait_recv()
-            return carry
-
-        lax.fori_loop(1, inner, take, 0)
-
-        def contract(s, carry):
+        def contract(d, carry):
+            s = lax.rem(place + d, inner)
+
+            @pl.when(d > 0)
+            def _():
+                c_copy(j, s, s).wait_recv()
+
             prod = lax.dot_general(cbuf[j, s], app[s], nt, preferred_element_type=jnp.float32)
             prod = jnp.where(same_pair, prod, 0.0)
             folded = prod[:, 0:128]
@@ -229,6 +229,12 @@
             recv_sem=r_recv.at[frm * slots + j], device_id=peer(line, to), device_id_type=MESH)
 
     def work(step, carry):
+        for k, (t, l) in events.items():
+            if t < outer - 1:
+                @pl.when(step == k)
+                def _():
+                    w_event(t, l)
+
         @pl.when(step < slots)
         def _():
             j = slot_at(step)
@@ -241,19 +247,15 @@
             lax.fori_loop(1, inner, take, 0)
             s_copy(j).start()
 
-        for l in range(1, local):
-            @pl.when(step == l - 1)
-            def _():
-                send_own(l)
-
         @pl.when(step + WINDOW < slots)
         def _():
             pack_step(step + WINDOW, 0)
 
         for k, (t, l) in events.items():
-            @pl.when(step == k)
-            def _():
-                w_event(t, l)
+            if t == outer - 1:
+                @pl.when(step == k)
+                def _():
+                    w_event(t, l)
 
         @pl.when(step > 1)
         def _():

time: 157 us -> 156 us (level)
  no operation moved by 1% of the time
where the time goes in v5:
time: 156 us
  Pallas kernels  152 us (97%)
  other arithmetic  3.05 us (2%)
  local copies, waits for them, and re-layouts  1.57 us (1%)
    pallas_call x1, Pallas kernels, body(): pl.pallas_call(functools.partial(kernel, outer, inner, local, cap, cap_pa...  152 us

profile of v5, /device:TPU:0, one launch (start us, length us, event | category | flops | bytes accessed | tf_op | source)
XLA Modules:
  0.0 156.2 jit_solution(7437262407504291370)
XLA Ops:
  0.0 0.9 convert_reduce_fusion
  0.9 0.8 select_reduce_fusion.1
  1.7 0.6 multiply_add_fusion
  2.3 0.7 select_reduce_fusion.source_row
  3.1 151.6 %shard_map.55 = f32[256,128]{1,0:T(8,128)} custom-call(s32[384]{0:T(512)} %select_reduce_fusion.source_row, s32[256]{0:T(256)} %get-tuple-element.5.target, bf16[256,16,512]{2,1,0:T(8,128)(2,1)} %val_hbm.1, bf16[256,16,512]{2,1,0:T(8,128)(2,1)} %cond_hbm.1, bf16[2,512,1024]{2,1,0:T(8,128)(2,1)} %w_hbm.1), custom_call_target="tpu_custom_call" | custom-call | flops 6442450944 | bytes 10485760 | tf_op jit(solution)/shard_map/pallas_call | solution.py:371
  154.7 1.6 %copy.7 = f32[256,128]{1,0:T(8,128)} copy(f32[256,128]{1,0:T(8,128)} %shard_map.55) | data formatting | bytes 262144
  (1 shorter events, 0.0 us)

commit v6 on v5

--- a/solution.py
+++ b/solution.py
@@ -97,9 +97,18 @@
         for i in range(cap):
             dst[i * bands:(i + 1) * bands, :] = src[source_row[first + i]]
 
+    def send_place(d):
+        if inner != 4:
+            return lax.rem(place + d, inner)
+        across_x = place + 1 - 2 * lax.rem(place, 2)
+        across_y = place + 2 - 4 * (place // 2)
+        first = jnp.where(core == 0, across_x, across_y)
+        second = jnp.where(core == 0, across_y, across_x)
+        return jnp.where(d == 1, first, jnp.where(d == 2, second, inner - 1 - place))
+
     def pack_val(j):
         def pack_to(d, carry):
-            to = lax.rem(place + d, inner)
+            to = send_place(d)
             fill(pack_v.at[to, j], val_in, (to * slots + j) * cap)
             v_copy(j, to, place).start()
             return carry
@@ -109,7 +118,7 @@
 
     def pack_cond(j):
         def pack_to(d, carry):
-            to = lax.rem(place + d, inner)
+            to = send_place(d)
             fill(pack_c.at[to, j], cond_in, (to * slots + j) * cap)
             c_copy(j, to, place).start()
             return carry

time: 156 us -> 156 us (level)
  no operation moved by 1% of the time
where the time goes in v6:
time: 156 us
  Pallas kernels  152 us (97%)
  other arithmetic  3.05 us (2%)
  local copies, waits for them, and re-layouts  1.57 us (1%)
    pallas_call x1, Pallas kernels, body(): pl.pallas_call(functools.partial(kernel, outer, inner, local, cap, cap_pa...  152 us

profile of v6, /device:TPU:0, one launch (start us, length us, event | category | flops | bytes accessed | tf_op | source)
XLA Modules:
  0.0 156.2 jit_solution(9667864742575149146)
XLA Ops:
  0.0 0.9 convert_reduce_fusion
  0.9 0.8 select_reduce_fusion.1
  1.7 0.6 multiply_add_fusion
  2.3 0.7 select_reduce_fusion.source_row
  3.1 151.6 %shard_map.55 = f32[256,128]{1,0:T(8,128)} custom-call(s32[384]{0:T(512)} %select_reduce_fusion.source_row, s32[256]{0:T(256)} %get-tuple-element.5.target, bf16[256,16,512]{2,1,0:T(8,128)(2,1)} %val_hbm.1, bf16[256,16,512]{2,1,0:T(8,128)(2,1)} %cond_hbm.1, bf16[2,512,1024]{2,1,0:T(8,128)(2,1)} %w_hbm.1), custom_call_target="tpu_custom_call" | custom-call | flops 6442450944 | bytes 10485760 | tf_op jit(solution)/shard_map/pallas_call | solution.py:380
  154.6 1.6 %copy.7 = f32[256,128]{1,0:T(8,128)} copy(f32[256,128]{1,0:T(8,128)} %shard_map.55) | data formatting | bytes 262144
  (1 shorter events, 0.0 us)

commit v7 on v5

--- a/solution.py
+++ b/solution.py
@@ -8,7 +8,7 @@
 from jax.sharding import PartitionSpec as P
 
 MESH = pl.DeviceIdType.MESH
-WINDOW = 3
+WINDOW = 2
 
 
 def kernel(outer, inner, local, cap, cap_pad, steps,

time: 156 us -> 157 us (level)
  no operation moved by 1% of the time
where the time goes in v7:
time: 157 us; the launch traced here: 156 us
  Pallas kernels  152 us (97%)
  other arithmetic  3.05 us (2%)
  local copies, waits for them, and re-layouts  1.57 us (1%)
    pallas_call x1, Pallas kernels, body(): pl.pallas_call(functools.partial(kernel, outer, inner, local, cap, cap_pa...  152 us

profile of v7, /device:TPU:0, one launch (start us, length us, event | category | flops | bytes accessed | tf_op | source)
XLA Modules:
  0.0 156.4 jit_solution(6482663081052840540)
XLA Ops:
  0.0 0.9 convert_reduce_fusion
  0.9 0.8 select_reduce_fusion.1
  1.7 0.6 multiply_add_fusion
  2.3 0.7 select_reduce_fusion.source_row
  3.1 151.8 %shard_map.55 = f32[256,128]{1,0:T(8,128)} custom-call(s32[384]{0:T(512)} %select_reduce_fusion.source_row, s32[256]{0:T(256)} %get-tuple-element.5.target, bf16[256,16,512]{2,1,0:T(8,128)(2,1)} %val_hbm.1, bf16[256,16,512]{2,1,0:T(8,128)(2,1)} %cond_hbm.1, bf16[2,512,1024]{2,1,0:T(8,128)(2,1)} %w_hbm.1), custom_call_target="tpu_custom_call" | custom-call | flops 6442450944 | bytes 10485760 | tf_op jit(solution)/shard_map/pallas_call | solution.py:371
  154.8 1.6 %copy.7 = f32[256,128]{1,0:T(8,128)} copy(f32[256,128]{1,0:T(8,128)} %shard_map.55) | data formatting | bytes 262144
  (1 shorter events, 0.0 us)
